TPU v7x, 256 devices: a whole 4x4x8 slice. The times are simulated.
256 devices in a mesh: smp: 8 (over x, core), proto: 32 (over z, y).
Axes of the slice: x: 4, y: 4, z: 8, core: 2. Of those that a mesh axis runs over, the one named last changes fastest.
Arguments:
- teacher_feats: float32 [4096, 384], P('smp'), may hold values from -11 to 11, as said below
- student_feats: float32 [4096, 384], P('smp'), may hold values from -15 to 15, as said below
- prototypes: float32 [384, 131072], P(None, 'proto'), may hold values from -0.25 to 0.25
Outputs:
- grad_feats: float32 [4096, 384], P('smp')
- grad_protos: float32 [384, 131072], P('smp', 'proto')
Inputs may be any that keep to these rules, and one draw needn't show every extreme that they name: `teacher_feats`: values of the teacher features of one crop. `student_feats`: values of the student features of one crop.
All inputs are finite; a program needn't handle non-finite values.
Results may differ from a plain program's by a relative error of at most 0.0003.
Values sent between devices are 32-bit elements; how exact they have to be, the bound alone decides.
A program may use at most 128 MiB of HBM per device.

v0:
```python
import jax
import jax.numpy as jnp
from jax import lax
from jax.sharding import PartitionSpec as P

ITERS = 3


teacher_temp = 0.07
student_temp = 0.1
highest = lax.Precision.HIGHEST


def local(teacher_feats, student_feats, prototypes):
    rows = teacher_feats.shape[0]
    teacher_scores = (
        jnp.dot(teacher_feats, prototypes, precision=highest, preferred_element_type=jnp.float32)
        / teacher_temp
    )
    peak = lax.pmax(jnp.max(teacher_scores, axis=0), "smp")
    expo = jnp.exp(teacher_scores - peak[None, :])
    crop_scale = jnp.ones((rows,), jnp.float32)
    proto_scale = jnp.ones((prototypes.shape[1],), jnp.float32)
    for step in range(ITERS):
        proto_scale = 1.0 / lax.psum(jnp.dot(crop_scale, expo, precision=highest), "smp")
        crop_scale = 1.0 / lax.psum(jnp.dot(expo, proto_scale, precision=highest), "proto")
    targets = crop_scale[:, None] * expo * proto_scale[None, :]
    student_scores = (
        jnp.dot(student_feats, prototypes, precision=highest, preferred_element_type=jnp.float32)
        / student_temp
    )
    local_top = jnp.max(student_scores, axis=1)
    row_top = lax.pmax(local_top, "proto")
    shifted = jnp.exp(student_scores - row_top[:, None])
    row_total = lax.psum(jnp.sum(shifted, axis=1), "proto")
    probs = shifted / row_total[:, None]
    dlogits = probs - targets
    feat_terms = (
        lax.dot_general(
            dlogits,
            prototypes,
            (((1,), (1,)), ((), ())),
            precision=highest,
            preferred_element_type=jnp.float32,
        )
        / student_temp
    )
    grad_feats = lax.psum(feat_terms, "proto")
    share = prototypes.shape[0] // lax.axis_size("smp")
    full_terms = (
        lax.dot_general(
            student_feats,
            dlogits,
            (((0,), (0,)), ((), ())),
            precision=highest,
            preferred_element_type=jnp.float32,
        )
        / student_temp
    )
    summed = lax.psum(full_terms, "smp")
    grad_protos = lax.dynamic_slice_in_dim(summed, lax.axis_index("smp") * share, share, 0)
    return (grad_feats, grad_protos)


def solution(mesh):
    in_specs = (P("smp", None), P("smp", None), P(None, "proto"))
    out_specs = (P("smp", None), P("smp", "proto"))
    return jax.shard_map(local, mesh=mesh, in_specs=in_specs, out_specs=out_specs, check_vma=False)
```

profile of v0, /device:TPU:1, one launch (start us, length us, event | category | flops | bytes accessed | tf_op | source)
XLA Modules:
  0.0 752.9 jit_solution(8634614060948915799)
XLA Ops:
  7.2 0.0 copy-start
  7.2 0.0 all-reduce.6.cloned.1.call-start
  7.2 17.6 %multiply_reduce_fusion = (f32[4096]{0:T(1024)S(1)}, f32[512,4096]{1,0:T(8,128)}) fusion(f32[512,384]{1,0:T(8,128)} %param.3, f32[384,4096]{1,0:T(8,128)} %param.5), kind=kOutput, calls=%fused_computation.3 | convolution fusion | flops 9667866624 | bytes 15482880 | tf_op jit(solution)/shard_map/dot_general | solution.py:17
  24.9 23.6 %pmax.15 = f32[4096]{0:T(1024)S(1)} all-reduce(f32[4096]{0:T(1024)S(1)} %get-tuple-element.6), channel_id=1, replica_groups=mesh['smp'=8,'proto'=32] {'smp'}, use_global_device_ids=true, to_apply=%region_5.0 | all-reduce | flops 4096 | bytes 32768 | tf_op jit(solution)/shard_map/pmax | solution.py:20
  48.4 7.3 fusion.1
  55.8 24.0 %psum.64 = f32[4096]{0:T(1024)S(1)} all-reduce(f32[4096]{0:T(1024)S(1)} %bitcast.33), channel_id=1, replica_groups=mesh['smp'=8,'proto'=32] {'smp'}, use_global_device_ids=true, to_apply=%region_6.0 | all-reduce | flops 4096 | bytes 32768 | tf_op jit(solution)/shard_map/psum | solution.py:25
  79.8 10.5 %fusion.8 = f32[1,512]{1,0:T(1,128)S(1)} fusion(f32[4096,1]{0,1:T(1,128)S(1)} %bitcast.29, f32[512,4096]{1,0:T(8,128)} %get-tuple-element.7, f32[4096]{0:T(1024)S(1)} %pmax.15), kind=kOutput, calls=%fused_computation.22 | convolution fusion | flops 29360128 | bytes 8423424 | tf_op jit(solution)/shard_map/dot_general | solution.py:26
  90.3 64.1 %psum.65 = f32[512]{0:T(512)S(1)} all-reduce(f32[512]{0:T(512)S(1)} %bitcast.35), channel_id=1, replica_groups=mesh['smp'=8,'proto'=32] {'proto'}, use_global_device_ids=true, to_apply=%region_7.0 | all-reduce | flops 512 | bytes 4096 | tf_op jit(solution)/shard_map/psum | solution.py:26
  154.4 7.4 fusion.7
  161.7 37.4 %psum.66 = f32[4096]{0:T(1024)S(1)} all-reduce(f32[4096]{0:T(1024)S(1)} %bitcast.30), channel_id=1, replica_groups=mesh['smp'=8,'proto'=32] {'smp'}, use_global_device_ids=true, to_apply=%region_8.0 | all-reduce | flops 4096 | bytes 32768 | tf_op jit(solution)/shard_map/psum | solution.py:25
  199.1 10.5 %fusion.6 = f32[1,512]{1,0:T(1,128)S(1)} fusion(f32[4096,1]{0,1:T(1,128)S(1)} %bitcast.31, f32[512,4096]{1,0:T(8,128)} %get-tuple-element.7, f32[4096]{0:T(1024)S(1)} %pmax.15), kind=kOutput, calls=%fused_computation.20 | convolution fusion | flops 29360128 | bytes 8423424 | tf_op jit(solution)/shard_map/dot_general | solution.py:26
  209.6 55.8 %psum.67 = f32[512]{0:T(512)S(1)} all-reduce(f32[512]{0:T(512)S(1)} %bitcast.37), channel_id=1, replica_groups=mesh['smp'=8,'proto'=32] {'proto'}, use_global_device_ids=true, to_apply=%region_9.0 | all-reduce | flops 512 | bytes 4096 | tf_op jit(solution)/shard_map/psum | solution.py:26
  265.4 0.0 slice-start
  265.4 7.5 fusion.5
  272.9 37.6 %psum.68 = f32[4096]{0:T(1024)S(1)} all-reduce(f32[4096]{0:T(1024)S(1)} %bitcast.32), channel_id=1, replica_groups=mesh['smp'=8,'proto'=32] {'smp'}, use_global_device_ids=true, to_apply=%region_10.0 | all-reduce | flops 4096 | bytes 32768 | tf_op jit(solution)/shard_map/psum | solution.py:25
  310.5 0.0 slice-start.1
  310.5 10.6 %fusion.4 = f32[1,512]{1,0:T(1,128)S(1)} fusion(f32[4096,1]{0,1:T(1,128)S(1)} %bitcast.28, f32[512,4096]{1,0:T(8,128)} %get-tuple-element.7, f32[4096]{0:T(1024)S(1)} %pmax.15), kind=kOutput, calls=%fused_computation.18 | convolution fusion | flops 29360128 | bytes 8423424 | tf_op jit(solution)/shard_map/dot_general | solution.py:26
  321.1 0.0 copy-done
  321.1 0.0 slice-done
  321.1 0.0 slice-done.1
  321.2 15.7 %multiply_reduce_fusion.1 = (f32[512]{0:T(512)S(1)}, f32[512,4096]{1,0:T(8,128)}) fusion(f32[512,384]{1,0:T(8,128)S(1)} %copy-done, f32[384,4096]{1,0:T(8,128)S(1)} %bitcast.27), kind=kOutput, calls=%fused_computation.4 | convolution fusion | flops 9667870720 | bytes 15468544 | tf_op jit(solution)/shard_map/dot_general | solution.py:29
  336.8 57.8 %pmax.14 = f32[512]{0:T(512)S(1)} all-reduce(f32[512]{0:T(512)S(1)} %get-tuple-element.8), channel_id=1, replica_groups=mesh['smp'=8,'proto'=32] {'proto'}, use_global_device_ids=true, to_apply=%region_1.0 | all-reduce | flops 512 | bytes 4096 | tf_op jit(solution)/shard_map/pmax | solution.py:33
  394.6 4.9 fusion
  399.4 56.3 %all-reduce = (f32[512]{0:T(512)S(1)}, f32[512]{0:T(512)S(1)}) all-reduce(f32[512]{0:T(512)S(1)} %bitcast.34, f32[512]{0:T(512)S(1)} %fusion), channel_id=1, replica_groups=mesh['smp'=8,'proto'=32] {'proto'}, use_global_device_ids=true, to_apply=%region_11.0 | all-reduce | flops 1024 | bytes 8192 | tf_op jit(solution)/shard_map/psum | solution.py:26
  455.7 7.8 %multiply_subtract_fusion = f32[512,4096]{1,0:T(8,128)S(1)} fusion(f32[512,4096]{1,0:T(8,128)} %get-tuple-element.9, f32[4096]{0:T(1024)S(1)} %broadcast_divide_fusion, f32[512]{0:T(512)S(1)} %broadcast_divide_fusion.5, f32[512]{0:T(512)S(1)} %get-tuple-element.5, f32[512]{0:T(512)S(1)} %pmax.14, f32[4096]{0:T(1024)S(1)} %pmax.15, f32[512,4096]{1,0:T(8,128)} %get-tuple-element.7), kind=kLoop, calls=%fused_computation | loop fusion | flops 16777216 | bytes 25204736 | tf_op jit(solution)/shard_map/sub | solution.py:37
  463.6 0.0 copy-start.1
  463.6 3.2 copy-done.1
  466.8 15.8 %multiply_bitcast_fusion = f32[384,4096]{0,1:T(8,128)} fusion(f32[512,4096]{1,0:T(8,128)S(1)} %multiply_subtract_fusion, f32[512,384]{1,0:T(8,128)S(1)} %copy-done), kind=kOutput, calls=%fused_computation.6 | convolution fusion | flops 9665249280 | bytes 15466496 | tf_op jit(solution)/shard_map/dot_general | solution.py:51
  482.5 0.0 all-reduce.6.cloned.1.call-update
  482.6 0.3 all-reduce.4.cloned.1.call-start
  482.9 17.7 %convolution_multiply_fusion = f32[512,384]{1,0:T(8,128)} fusion(f32[512,4096]{1,0:T(8,128)} %copy-done.1, f32[384,4096]{1,0:T(8,128)} %param.5), kind=kOutput, calls=%fused_computation.7 | convolution fusion | flops 9663873024 | bytes 15466496 | tf_op jit(solution)/shard_map/dot_general | solution.py:39
  500.5 0.0 all-reduce.4.cloned.1.call-update
  500.6 95.0 %all-reduce.6.cloned.1.call-done = f32[384,4096]{0,1:T(8,128)} async-done(((f32[384,4096]{0,1:T(8,128)}), f32[384,4096]{0,1:T(8,128)}) %all-reduce.6.cloned.1.call-update) | async-done | bytes 6291472 | tf_op jit(solution)/shard_map/psum | solution.py:60
  595.5 2.8 constant_dynamic-slice_fusion
  598.3 1.5 copy.5
  599.8 143.8 %all-reduce.4.cloned.1.call-done = f32[512,384]{1,0:T(8,128)} async-done(((f32[512,384]{1,0:T(8,128)}), f32[512,384]{1,0:T(8,128)}) %all-reduce.4.cloned.1.call-update) | async-done | bytes 786448 | tf_op jit(solution)/shard_map/psum | solution.py:48
  743.6 2.1 copy.8
  (7 shorter events, 0.0 us)
Async XLA Ops:
  7.2 314.0 %copy-start = (f32[512,384]{1,0:T(8,128)S(1)}, f32[512,384]{1,0:T(8,128)}, u32[]{:S(2)}) copy-start(f32[512,384]{1,0:T(8,128)} %param.4) | copy-start | bytes 2359300
  7.2 588.3 %all-reduce.6.cloned.1.call-start = ((), (), s32[]{:S(2)}) async-start(), calls=%async_computation.1 | async-start | bytes 12582912 | tf_op jit(solution)/shard_map/psum | solution.py:60
  265.4 55.8 %slice-start = ((s8[6291456]{0:T(1024)(128)(4,1)}), s8[2097152]{0:T(1024)(128)(4,1)S(1)}, s32[]{:S(2)}) async-start(s8[6291456]{0:T(1024)(128)(4,1)} %bitcast.26), calls=%async_computation.2 | async-start | bytes 4194304
  310.5 10.7 %slice-start.1 = ((s8[6291456]{0:T(1024)(128)(4,1)}), s8[4194304]{0:T(1024)(128)(4,1)S(1)}, s32[]{:S(2)}) async-start(s8[6291456]{0:T(1024)(128)(4,1)} %bitcast.26), calls=%async_computation.3 | async-start | bytes 8388608
  463.6 3.2 copy-start.1
  482.6 261.0 %all-reduce.4.cloned.1.call-start = ((), (), s32[]{:S(2)}) async-start(), calls=%async_computation | async-start | bytes 1572864 | tf_op jit(solution)/shard_map/psum | solution.py:48
Sparse Core Ops, SparseCore 0:
  482.7 112.8 all-reduce.5
  599.5 144.0 all-reduce.3
where the time goes:
time: 764 us; the launch traced here: 753 us
  blocking collectives  356 us (47%)
  waiting for transfers between devices  239 us (31%)
  matrix products  120 us (16%)
  between operations  14.6 us (2%)
  other arithmetic  12.7 us (2%)
  local copies, waits for them, and re-layouts  9.55 us (1%)
    psum x3, blocking collectives, local(): lax.psum(jnp.dot(expo, proto_scale, precision=highest), 'proto')  176 us
    psum x1, waiting for transfers between devices, local(): grad_feats = lax.psum(feat_terms, 'proto')  144 us
    psum x3, blocking collectives, local(): lax.psum(jnp.dot(crop_scale, expo, precision=highest), 'smp')  99.1 us
    psum x1, waiting for transfers between devices, local(): summed = lax.psum(full_terms, 'smp')  95 us
    pmax x1, blocking collectives, local(): row_top = lax.pmax(local_top, 'proto')  57.8 us
    dot_general x3, matrix products, local(): jnp.dot(expo, proto_scale, precision=highest)  31.6 us
    pmax x1, blocking collectives, local(): peak = lax.pmax(jnp.max(teacher_scores, axis=0), 'smp')  23.6 us
    dot_general x3, matrix products, local(): jnp.dot(crop_scale, expo, precision=highest)  22.2 us
  transfers between devices with their start and end apart: 2, of which 2 were waited for; matrix products, arithmetic and copies ran while one was open for 3% of the time, Pallas kernels for 0%

commit v1 on v0

v1 whole, which is shorter than its diff:
```python
import functools

import jax
import jax.numpy as jnp
from jax import lax
from jax.experimental import pallas as pl
from jax.experimental.pallas import tpu as pltpu
from jax.sharding import PartitionSpec as P

ITERS = 3
TEACHER_TEMP = 0.07
STUDENT_TEMP = 0.1
LOG2E = 1.4426950408889634

YN = 4
TILE = 512
LANES = 128
MESH = pl.DeviceIdType.MESH
f32 = jnp.float32
bf16 = jnp.bfloat16


def mm(a, b):
    return jnp.dot(a, b, preferred_element_type=f32)


def mm_t(a, b):
    return lax.dot_general(a, b, (((1,), (1,)), ((), ())), preferred_element_type=f32)


def split(v):
    hi = v.astype(bf16)
    return hi, (v - hi.astype(f32)).astype(bf16)


def kernel(
    SN,
    PN,
    t_hbm,
    s_hbm,
    p_hbm,
    gf_out,
    gp_out,
    feats,
    thh,
    tl,
    shh,
    sl,
    st,
    phl,
    e,
    q,
    dh,
    dl,
    cola,
    cola_in,
    col,
    col_in,
    pscale,
    peakf,
    acc,
    mx,
    cb,
    ab,
    rowm,
    row_y,
    row_z,
    rowt,
    stat,
    stat_y,
    stat_t,
    stat_z,
    gfacc,
    gfs,
    gfy,
    gfz,
    gft,
    gfz2,
    cr,
    xa,
    xb,
    load_sem,
    cs_sem,
    cr_sem,
    rys_sem,
    ryr_sem,
    rzs_sem,
    rzr_sem,
    sts_sem,
    str_sem,
    gs_sem,
    gr_sem,
    ks_sem,
    kr_sem,
    xs_sem,
    xr_sem,
):
    ZN = PN // YN
    XN = SN // 2
    rows, width = t_hbm.shape
    tiles = p_hbm.shape[1] // TILE
    per = TILE // LANES
    blocks = rows // LANES
    s = lax.axis_index("smp")
    p = lax.axis_index("proto")
    x = s // 2
    c = s % 2
    z = p // YN
    y = p % YN
    sibling = (2 * x + 1 - c, p)
    right = (2 * ((x + 1) % XN) + c, p)
    left = (2 * ((x + XN - 1) % XN) + c, p)
    smp_peers = [((s + d) % SN, p) for d in range(1, SN)]
    y_peers = [(s, z * YN + (y + d) % YN) for d in range(1, YN)]
    z_peers = [(s, ((z + d) % ZN) * YN + y) for d in range(1, ZN)]

    def rc(src, dst, ss, rs, dev):
        return pltpu.make_async_remote_copy(
            src_ref=src, dst_ref=dst, send_sem=ss, recv_sem=rs, device_id=dev, device_id_type=MESH
        )

    barrier = pltpu.get_barrier_semaphore()
    for dev in smp_peers + y_peers + z_peers:
        pl.semaphore_signal(barrier, inc=1, device_id=dev, device_id_type=MESH)

    load_t = pltpu.make_async_copy(t_hbm, feats.at[0], load_sem.at[0])
    load_s = pltpu.make_async_copy(s_hbm, feats.at[1], load_sem.at[1])

    def load_p(j):
        cols = pl.ds(pl.multiple_of(j * TILE, TILE), TILE)
        return pltpu.make_async_copy(
            p_hbm.at[:, cols], q.at[j, pl.ds(0, width)], load_sem.at[2 + j]
        )

    load_t.start()
    for j in range(tiles):
        load_p(j).start()
    load_s.start()

    def group_send(src, dst, me, peers, ssem, rsem, n):
        for d, dev in enumerate(peers):
            rc(src(d), dst.at[me], ssem.at[d], rsem.at[me], dev).start()

    def group_wait(src, dst, me, peers, ssem, rsem, n):
        for d, dev in enumerate(peers):
            other = (me + d + 1) % n
            copy = rc(src(d), dst.at[other], ssem.at[d], rsem.at[other], dev)
            copy.wait_recv()
            copy.wait_send()

    load_t.wait()
    hi, lo = split(feats[0] * (LOG2E / (TEACHER_TEMP / STUDENT_TEMP)))
    thh[:, 0:width] = hi
    thh[:, width : 2 * width] = hi
    tl[...] = lo

    @pl.loop(0, tiles)
    def _(j):
        load_p(j).wait()
        ph, plo = split(q[j, 0:width, :] * (1.0 / STUDENT_TEMP))
        phl[j, 0:width, :] = ph
        phl[j, width : 2 * width, :] = plo
        scores = mm(thh[...], phl[j]) + mm(tl[...], phl[j, 0:width, :])
        top = jnp.max(scores, axis=0, keepdims=True)
        ex = jnp.exp2(scores - top)
        e[j] = ex
        total = jnp.sum(ex, axis=0, keepdims=True)
        for i in range(per):
            cola[pl.ds(per * j + i, 1), :] = top[:, LANES * i : LANES * (i + 1)]
            cola[pl.ds(per * (tiles + j) + i, 1), :] = total[:, LANES * i : LANES * (i + 1)]

    pl.semaphore_wait(barrier, len(smp_peers) + len(y_peers) + len(z_peers))

    def student(first, last):
        @pl.loop(first, last)
        def _(j):
            scores = mm(shh[...], phl[j]) + mm(sl[...], phl[j, 0:width, :])
            q[j] = scores
            for r in range(blocks):
                rs = slice(LANES * r, LANES * (r + 1))
                m = mx[rs, :]
                for i in range(per):
                    m = jnp.maximum(m, scores[rs, LANES * i : LANES * (i + 1)])
                mx[rs, :] = m

    def student_start():
        load_s.wait()
        sf = feats[1]
        shi, slo = split(sf * LOG2E)
        shh[:, 0:width] = shi
        shh[:, width : 2 * width] = shi
        sl[...] = slo
        mx[...] = jnp.full(mx.shape, -jnp.inf, f32)

    def student_transpose():
        keep = width // SN
        ht, lt = split((feats[1] * (1.0 / STUDENT_TEMP)).T)
        for core in range(2):
            for chip in range(XN):
                to = (core * XN + chip) * keep
                fr = (2 * chip + core) * keep
                st[0, to : to + keep, :] = ht[fr : fr + keep, :]
                st[1, to : to + keep, :] = lt[fr : fr + keep, :]

    def to_rows(ref, reduce, out, base):
        for r in range(blocks):
            rs = slice(LANES * r, LANES * (r + 1))
            out[base + r : base + r + 1, :] = reduce(ref[rs, :].T, axis=0, keepdims=True)

    def to_columns(v, out):
        for r in range(blocks):
            rs = slice(LANES * r, LANES * (r + 1))
            out[rs, :] = jnp.broadcast_to(v[r : r + 1, :], (LANES, LANES)).T

    def student_totals():
        to_rows(mx, jnp.max, stat, 0)
        to_columns(stat[0:blocks, :], ab)
        mx[...] = jnp.zeros(mx.shape, f32)

        @pl.loop(0, tiles)
        def _(j):
            for r in range(blocks):
                rs = slice(LANES * r, LANES * (r + 1))
                m = ab[rs, :]
                a = mx[rs, :]
                for i in range(per):
                    ls = slice(LANES * i, LANES * (i + 1))
                    v = jnp.exp2(q[j, rs, ls] - m)
                    q[j, rs, ls] = v
                    a = a + v
                mx[rs, :] = a

        to_rows(mx, jnp.sum, stat, blocks)

    def combine(ref):
        tops = [ref[k, 0:blocks, :] for k in range(ref.shape[0])]
        top = functools.reduce(jnp.maximum, tops)
        total = sum(ref[k, blocks : 2 * blocks, :] * jnp.exp2(tops[k] - top) for k in range(ref.shape[0]))
        return top, total

    def row_pass(it):
        acc[...] = jnp.zeros(acc.shape, f32)

        @pl.loop(0, tiles)
        def _(j):
            ws = [pscale[pl.ds(per * j + i, 1), :] for i in range(per)]
            fs = [peakf[pl.ds(per * j + i, 1), :] for i in range(per)] if it == 0 else None
            for r in range(blocks):
                rs = slice(LANES * r, LANES * (r + 1))
                a = acc[rs, :]
                for i in range(per):
                    ls = slice(LANES * i, LANES * (i + 1))
                    v = e[j, rs, ls]
                    if it == 0:
                        v = v * fs[i]
                        e[j, rs, ls] = v
                    a = a + v * ws[i]
                acc[rs, :] = a

        to_rows(acc, jnp.sum, rowm.at[it], 0)

    def row_start(it):
        row_y[it, pl.ds(y, 1)] = rowm[it : it + 1]
        group_send(lambda d: rowm.at[it], row_y.at[it], y, y_peers, rys_sem.at[it], ryr_sem.at[it], YN)

    def row_middle(it):
        group_wait(lambda d: rowm.at[it], row_y.at[it], y, y_peers, rys_sem.at[it], ryr_sem.at[it], YN)
        rowt[it] = sum(row_y[it, k] for k in range(YN))
        row_z[it, pl.ds(z, 1)] = rowt[it : it + 1]
        group_send(lambda d: rowt.at[it], row_z.at[it], z, z_peers, rzs_sem.at[it], rzr_sem.at[it], ZN)

    def row_end(it):
        group_wait(lambda d: rowt.at[it], row_z.at[it], z, z_peers, rzs_sem.at[it], rzr_sem.at[it], ZN)
        mass = sum(row_z[it, k] for k in range(ZN))
        to_columns(1.0 / mass, cb)

    def col_pass(it):
        @pl.loop(0, tiles)
        def _(j):
            for i in range(per):
                ls = slice(LANES * i, LANES * (i + 1))
                v = jnp.sum(e[j, :, ls] * cb[...], axis=0, keepdims=True)
                col[it, pl.ds(per * j + i, 1), :] = v

    def col_start(it):
        col_in[it, pl.ds(s, 1)] = col[it : it + 1]
        group_send(lambda d: col.at[it], col_in.at[it], s, smp_peers, cs_sem.at[it + 1], cr_sem.at[it + 1], SN)

    def col_end(it):
        group_wait(lambda d: col.at[it], col_in.at[it], s, smp_peers, cs_sem.at[it + 1], cr_sem.at[it + 1], SN)
        pscale[...] = 1.0 / sum(col_in[it, k] for k in range(SN))

    half = per * tiles
    cola_in[pl.ds(s, 1)] = cola[...][None]
    group_send(lambda d: cola, cola_in, s, smp_peers, cs_sem.at[0], cr_sem.at[0], SN)
    student_start()
    student(0, tiles // 4)
    group_wait(lambda d: cola, cola_in, s, smp_peers, cs_sem.at[0], cr_sem.at[0], SN)
    tops = [cola_in[k, 0:half, :] for k in range(SN)]
    top = functools.reduce(jnp.maximum, tops)
    pscale[...] = 1.0 / sum(cola_in[k, half : 2 * half, :] * jnp.exp2(tops[k] - top) for k in range(SN))
    peakf[...] = jnp.exp2(cola[0:half, :] - top)

    row_pass(0)
    row_start(0)
    student(tiles // 4, tiles // 2)
    row_middle(0)
    student(tiles // 2, 3 * tiles // 4)
    row_end(0)
    col_pass(0)
    col_start(0)
    student(3 * tiles // 4, tiles)
    col_end(0)

    row_pass(1)
    row_start(1)
    student_totals()
    stat_y[pl.ds(y, 1)] = stat[...][None]
    group_send(lambda d: stat, stat_y, y, y_peers, sts_sem.at[0], str_sem.at[0], YN)
    row_middle(1)
    student_transpose()
    row_end(1)
    col_pass(1)
    col_start(1)
    group_wait(lambda d: stat, stat_y, y, y_peers, sts_sem.at[0], str_sem.at[0], YN)
    top, total = combine(stat_y)
    stat_t[0:blocks, :] = top
    stat_t[blocks : 2 * blocks, :] = total
    stat_z[pl.ds(z, 1)] = stat_t[...][None]
    group_send(lambda d: stat_t, stat_z, z, z_peers, sts_sem.at[1], str_sem.at[1], ZN)
    gfacc[...] = jnp.zeros(gfacc.shape, f32)
    col_end(1)

    row_pass(2)
    row_start(2)
    group_wait(lambda d: stat_t, stat_z, z, z_peers, sts_sem.at[1], str_sem.at[1], ZN)
    top, total = combine(stat_z)
    to_columns(jnp.exp2(stat[0:blocks, :] - top) / total, ab)
    row_middle(2)
    row_end(2)

    @pl.loop(0, tiles)
    def _(j):
        for i in range(per):
            ls = slice(LANES * i, LANES * (i + 1))
            w = pscale[pl.ds(per * j + i, 1), :]
            d = q[j, :, ls] * ab[...] - (cb[...] * e[j, :, ls]) * w
            dhi, dlo = split(d)
            dh[j, :, ls] = dhi
            dl[j, :, ls] = dlo
        gfacc[...] += mm_t(dh[j], phl[j])
        gfacc[:, 0:width] += mm_t(dl[j], phl[j, 0:width, :])

    part = rows // YN
    piece = part // ZN
    for k in range(YN):
        rs = slice(k * part, (k + 1) * part)
        gfs[k] = gfacc[rs, 0:width] + gfacc[rs, width : 2 * width]

    def ypeer(d):
        return (y + d + 1) % YN

    def zpeer(d):
        return (z + d + 1) % ZN

    def gf_a():
        group_send(lambda d: gfs.at[ypeer(d)], gfy, y, y_peers, gs_sem.at[0], gr_sem.at[0], YN)

    def gf_b():
        group_wait(lambda d: gfs.at[ypeer(d)], gfy, y, y_peers, gs_sem.at[0], gr_sem.at[0], YN)
        gfy[pl.ds(y, 1)] = gfs[pl.ds(y, 1)]
        v = sum(gfy[k] for k in range(YN))
        for k in range(ZN):
            gft[k] = v[k * piece : (k + 1) * piece]
        group_send(lambda d: gft.at[zpeer(d)], gfz, z, z_peers, gs_sem.at[1], gr_sem.at[1], ZN)

    def gf_c():
        group_wait(lambda d: gft.at[zpeer(d)], gfz, z, z_peers, gs_sem.at[1], gr_sem.at[1], ZN)
        gfz[pl.ds(z, 1)] = gft[pl.ds(z, 1)]
        gfz2[pl.ds(z, 1)] = sum(gfz[k] for k in range(ZN))[None]
        group_send(lambda d: gfz2.at[z], gfz2, z, z_peers, gs_sem.at[2], gr_sem.at[2], ZN)

    def gf_d():
        group_wait(lambda d: gfz2.at[z], gfz2, z, z_peers, gs_sem.at[2], gr_sem.at[2], ZN)
        mine = pl.multiple_of(y * part, part)
        for k in range(ZN):
            gf_out[pl.ds(pl.multiple_of(mine + k * piece, piece), piece), :] = gfz2[k]
        for d, dev in enumerate(y_peers):
            block = gf_out.at[pl.ds(mine, part)]
            rc(block, block, gs_sem.at[3, d], gr_sem.at[3, y], dev).start()

    def gf_e():
        mine = pl.multiple_of(y * part, part)
        for d, dev in enumerate(y_peers):
            block = gf_out.at[pl.ds(mine, part)]
            theirs = gf_out.at[pl.ds(pl.multiple_of(ypeer(d) * part, part), part)]
            copy = rc(block, theirs, gs_sem.at[3, d], gr_sem.at[3, ypeer(d)], dev)
            copy.wait_recv()
            copy.wait_send()

    gf_a()

    keep = width // SN
    hk = keep // 2
    mine = pl.multiple_of(c * (width // 2), width // 2)
    other = pl.multiple_of((1 - c) * (width // 2), width // 2)
    across = pl.multiple_of(((x + 2) % XN) * keep, keep)
    ahead = pl.multiple_of(((x + 1) % XN) * keep, keep)
    behind = pl.multiple_of(((x + XN - 1) % XN) * keep, keep)
    here = pl.multiple_of(x * keep, keep)

    def core_copy(t):
        return rc(e.at[t, pl.ds(other, width // 2)], cr.at[t], ks_sem.at[t], kr_sem.at[t], sibling)

    def x_copy(t, k):
        row, dst, dev = [
            (across, xa.at[t, 0], right),
            (across + hk, xa.at[t, 1], left),
            (ahead + hk, xb.at[t, 0, pl.ds(hk, hk)], right),
            (behind, xb.at[t, 1, pl.ds(0, hk)], left),
            (ahead, xb.at[t, 0, pl.ds(0, hk)], right),
            (behind + hk, xb.at[t, 1, pl.ds(hk, hk)], left),
        ][k]
        src = cr.at[t, pl.ds(pl.multiple_of(row, 8), hk)]
        return rc(src, dst, xs_sem.at[t, k], xr_sem.at[t, k], dev)

    lag_core, lag_a, lag_b = 1, 3, 5

    @pl.loop(0, tiles + lag_b)
    def _(i):
        @pl.when(i < tiles)
        def _():
            d = dh[i]
            e[i, 0:width, :] = mm(st[0], d) + mm(st[1], d) + mm(st[0], dl[i])
            core_copy(i).start()

        @pl.when((i >= lag_core) & (i < tiles + lag_core))
        def _():
            t = i - lag_core
            core_copy(t).wait_recv()
            cr[t] = cr[t] + e[t, pl.ds(mine, width // 2), :]
            for k in range(4):
                x_copy(t, k).start()

        @pl.when((i >= lag_a) & (i < tiles + lag_a))
        def _():
            t = i - lag_a
            x_copy(t, 0).wait_recv()
            x_copy(t, 1).wait_recv()
            a = pl.ds(pl.multiple_of(ahead, 8), hk)
            cr[t, a, :] = cr[t, a, :] + xa[t, 0]
            b = pl.ds(pl.multiple_of(behind + hk, 8), hk)
            cr[t, b, :] = cr[t, b, :] + xa[t, 1]
            x_copy(t, 4).start()
            x_copy(t, 5).start()

        @pl.when(i >= lag_b)
        def _():
            t = i - lag_b
            for k in range(2, 6):
                x_copy(t, k).wait_recv()
            cols = pl.ds(pl.multiple_of(t * TILE, TILE), TILE)
            gp_out[:, cols] = cr[t, pl.ds(here, keep), :] + xb[t, 0] + xb[t, 1]
            core_copy(t).wait_send()
            for k in range(6):
                x_copy(t, k).wait_send()

        @pl.when(i == 5)
        def _():
            gf_b()

        @pl.when(i == 7)
        def _():
            gf_c()

        @pl.when(i == 9)
        def _():
            gf_d()

    gf_e()


def local(SN, PN, teacher_feats, student_feats, prototypes):
    rows, width = teacher_feats.shape
    protos = prototypes.shape[1]
    tiles = protos // TILE
    half = protos // LANES
    blocks = rows // LANES
    ZN = PN // YN
    part = rows // YN
    piece = part // ZN
    V = pltpu.VMEM
    DMA = pltpu.SemaphoreType.DMA
    scratch = [
        V((2, rows, width), f32),
        V((rows, 2 * width), bf16),
        V((rows, width), bf16),
        V((rows, 2 * width), bf16),
        V((rows, width), bf16),
        V((2, width, rows), bf16),
        V((tiles, 2 * width, TILE), bf16),
        V((tiles, rows, TILE), f32),
        V((tiles, rows, TILE), f32),
        V((tiles, rows, TILE), bf16),
        V((tiles, rows, TILE), bf16),
        V((2 * half, LANES), f32),
        V((SN, 2 * half, LANES), f32),
        V((ITERS - 1, half, LANES), f32),
        V((ITERS - 1, SN, half, LANES), f32),
        V((half, LANES), f32),
        V((half, LANES), f32),
        V((rows, LANES), f32),
        V((rows, LANES), f32),
        V((rows, LANES), f32),
        V((rows, LANES), f32),
        V((ITERS, blocks, LANES), f32),
        V((ITERS, YN, blocks, LANES), f32),
        V((ITERS, ZN, blocks, LANES), f32),
        V((ITERS, blocks, LANES), f32),
        V((2 * blocks, LANES), f32),
        V((YN, 2 * blocks, LANES), f32),
        V((2 * blocks, LANES), f32),
        V((ZN, 2 * blocks, LANES), f32),
        V((rows, 2 * width), f32),
        V((YN, part, width), f32),
        V((YN, part, width), f32),
        V((ZN, piece, width), f32),
        V((ZN, piece, width), f32),
        V((ZN, piece, width), f32),
        V((tiles, width // 2, TILE), f32),
        V((tiles, 2, width // SN // 2, TILE), f32),
        V((tiles, 2, width // SN, TILE), f32),
        DMA((2 + tiles,)),
        DMA((ITERS, SN - 1)),
        DMA((ITERS, SN)),
        DMA((ITERS, YN - 1)),
        DMA((ITERS, YN)),
        DMA((ITERS, ZN - 1)),
        DMA((ITERS, ZN)),
        DMA((2, ZN - 1)),
        DMA((2, ZN)),
        DMA((4, ZN - 1)),
        DMA((4, ZN)),
        DMA((tiles,)),
        DMA((tiles,)),
        DMA((tiles, 6)),
        DMA((tiles, 6)),
    ]
    flops = 2 * rows * width * protos
    return pl.pallas_call(
        functools.partial(kernel, SN, PN),
        out_shape=(
            jax.ShapeDtypeStruct((rows, width), f32),
            jax.ShapeDtypeStruct((width // SN, protos), f32),
        ),
        in_specs=[pl.BlockSpec(memory_space=pl.ANY)] * 3,
        out_specs=(pl.BlockSpec(memory_space=pltpu.VMEM), pl.BlockSpec(memory_space=pltpu.VMEM)),
        scratch_shapes=scratch,
        compiler_params=pltpu.CompilerParams(
            collective_id=0, has_side_effects=True, vmem_limit_bytes=62 * 1024 * 1024
        ),
        cost_estimate=pl.CostEstimate(
            flops=12 * flops, bytes_accessed=4 * width * (protos + 4 * rows), transcendentals=2 * rows * protos
        ),
    )(teacher_feats, student_feats, prototypes)


def solution(mesh):
    SN, PN = mesh.shape["smp"], mesh.shape["proto"]
    in_specs = (P("smp", None), P("smp", None), P(None, "proto"))
    out_specs = (P("smp", None), P("smp", "proto"))
    return jax.shard_map(
        functools.partial(local, SN, PN), mesh=mesh, in_specs=in_specs, out_specs=out_specs, check_vma=False
    )
```

time: 764 us -> 113 us (0.15); the launches traced: 753 us -> 113 us
  blocking collectives: 356 us -> 0 us
  waiting for transfers between devices: 239 us -> 0 us
  matrix products: 120 us -> 0 us
  Pallas kernels: 0 us -> 108 us
  between operations: 14.6 us -> 0.64 us
  other arithmetic: 12.7 us -> 0 us
    psum x6 -> x0, blocking collectives: 275 us -> none  [the longest x3 176 us: local(): lax.psum(jnp.dot(expo, proto_scale, precision=highest), 'proto')]
    psum x2 -> x0, waiting for transfers between devices: 239 us -> none  [the longest x1 144 us: local(): grad_feats = lax.psum(feat_terms, 'proto')]
    dot_general x10 -> x0, matrix products: 120 us -> none  [the longest x3 31.6 us: local(): jnp.dot(expo, proto_scale, precision=highest)]
    pallas_call x0 -> x1, Pallas kernels: none -> 108 us  [local(): pl.pallas_call(functools.partial(kernel, SN, PN), out_shape=(jax.ShapeDty...]
    pmax x2 -> x0, blocking collectives: 81.3 us -> none  [the longest x1 57.8 us: local(): row_top = lax.pmax(local_top, 'proto')]
    sub x1 -> x0, other arithmetic: 7.84 us -> none  [local(): dlogits = probs - targets]
  transfers between devices with their start and end apart: 2 -> 0, of which waited for: 2 -> 0; matrix products, arithmetic and copies ran while one was open for 3% -> 0% of each run, Pallas kernels for 0% -> 0%
where the time goes in v1:
time: 113 us
  Pallas kernels  108 us (96%)
  local copies, waits for them, and re-layouts  4.13 us (4%)
    pallas_call x1, Pallas kernels, local(): pl.pallas_call(functools.partial(kernel, SN, PN), out_shape=(jax.ShapeDty...  108 us
    unnamed x2, local copies, waits for them, and re-layouts  4.13 us

profile of v1, /device:TPU:1, one launch (start us, length us, event | category | flops | bytes accessed | tf_op | source)
XLA Modules:
  0.0 112.5 jit_solution(11143407550783387703)
XLA Ops:
  0.6 107.7 %shard_map.50 = (f32[512,384]{1,0:T(8,128)}, f32[48,4096]{1,0:T(8,128)}) custom-call(f32[512,384]{1,0:T(8,128)} %t_hbm.1, f32[512,384]{1,0:T(8,128)} %s_hbm.1, f32[384,4096]{1,0:T(8,128)} %p_hbm.1), custom_call_target="tpu_custom_call" | custom-call | flops 19327352832 | bytes 9437184 | tf_op jit(solution)/shard_map/pallas_call | solution.py:550
  108.4 2.1 %copy.7 = f32[512,384]{1,0:T(8,128)} copy(f32[512,384]{1,0:T(8,128)} %get-tuple-element.4) | data formatting | bytes 1572864
  110.4 2.1 %copy.8 = f32[48,4096]{1,0:T(8,128)} copy(f32[48,4096]{1,0:T(8,128)} %get-tuple-element.5) | data formatting | bytes 1572864

commit v2 on v1

v2 whole, which is shorter than its diff:
```python
import functools

import jax
import jax.numpy as jnp
from jax import lax
from jax.experimental import pallas as pl
from jax.experimental.pallas import tpu as pltpu
from jax.sharding import PartitionSpec as P

ITERS = 3
TEACHER_TEMP = 0.07
STUDENT_TEMP = 0.1
LOG2E = 1.4426950408889634

YN = 4
TILE = 512
LANES = 128
MESH = pl.DeviceIdType.MESH
f32 = jnp.float32
bf16 = jnp.bfloat16


def mm(a, b):
    return jnp.dot(a, b, preferred_element_type=f32)


def mm_t(a, b):
    return lax.dot_general(a, b, (((1,), (1,)), ((), ())), preferred_element_type=f32)


def split(v):
    hi = v.astype(bf16)
    return hi, (v - hi.astype(f32)).astype(bf16)


def kernel(
    SN,
    PN,
    t_hbm,
    s_hbm,
    p_hbm,
    gf_out,
    gp_out,
    feats,
    thh,
    tl,
    shh,
    sl,
    st,
    phl,
    e,
    q,
    dh,
    dl,
    cola,
    cola_in,
    col,
    col_in,
    pscale,
    peakf,
    acc,
    mx,
    cb,
    ab,
    rowm,
    row_in,
    stat,
    stat_in,
    gfacc,
    gfs,
    gya,
    gyb,
    gfz,
    gft,
    gfz2,
    gfo,
    cr,
    xa,
    xb,
    gpo,
    load_sem,
    cs_sem,
    cr_sem,
    rs_sem,
    rr_sem,
    st_sem,
    ys_sem,
    yr_sem,
    zs_sem,
    zr_sem,
    ks_sem,
    kr_sem,
    xs_sem,
    xr_sem,
    out_sem,
):
    ZN = PN // YN
    XN = SN // 2
    rows, width = t_hbm.shape
    tiles = p_hbm.shape[1] // TILE
    per = TILE // LANES
    blocks = rows // LANES
    s = lax.axis_index("smp")
    p = lax.axis_index("proto")
    x = s // 2
    c = s % 2
    z = p // YN
    y = p % YN
    sibling = (2 * x + 1 - c, p)
    right = (2 * ((x + 1) % XN) + c, p)
    left = (2 * ((x + XN - 1) % XN) + c, p)
    y_right = (s, z * YN + (y + 1) % YN)
    y_left = (s, z * YN + (y + YN - 1) % YN)

    def far(d, n):
        return min(d, n - d)

    offsets = sorted(((dx, dc) for dx in range(XN) for dc in range(2)), key=lambda o: -far(o[0], XN))
    smp_peers = [2 * ((x + dx) % XN) + (c + dc) % 2 for dx, dc in offsets if dx or dc]
    smp_group = (s, SN, [(k, (k, p)) for k in smp_peers])
    offsets = sorted(((dz, dy) for dz in range(ZN) for dy in range(YN)), key=lambda o: -far(o[0], ZN) - far(o[1], YN))
    row_peers = [((z + dz) % ZN) * YN + (y + dy) % YN for dz, dy in offsets if dz or dy]
    row_group = (p, PN, [(k, (s, k)) for k in row_peers])
    z_peers = [(z + dz) % ZN for dz in sorted(range(1, ZN), key=lambda d: -far(d, ZN))]
    z_group = (z, ZN, [(k, (s, k * YN + y)) for k in z_peers])

    def rc(src, dst, ss, rs, dev):
        return pltpu.make_async_remote_copy(
            src_ref=src, dst_ref=dst, send_sem=ss, recv_sem=rs, device_id=dev, device_id_type=MESH
        )

    barrier = pltpu.get_barrier_semaphore()
    for _, dev in smp_group[2] + row_group[2]:
        pl.semaphore_signal(barrier, inc=1, device_id=dev, device_id_type=MESH)

    load_t = pltpu.make_async_copy(t_hbm, feats.at[0], load_sem.at[0])
    load_s = pltpu.make_async_copy(s_hbm, feats.at[1], load_sem.at[1])

    def load_p(j):
        cols = pl.ds(pl.multiple_of(j * TILE, TILE), TILE)
        return pltpu.make_async_copy(
            p_hbm.at[:, cols], q.at[j, pl.ds(0, width)], load_sem.at[2 + j]
        )

    load_t.start()
    for j in range(tiles):
        load_p(j).start()
    load_s.start()

    def group_send(src, dst, group, ssem, rsem):
        me, n, peers = group
        for k, dev in peers:
            rc(src(k), dst.at[me], ssem, rsem, dev).start()

    def group_wait(dst, group, ssem, rsem):
        me, n, peers = group
        blocks = dst.at[pl.ds(0, n - 1)]
        copy = rc(blocks, blocks, ssem, rsem, peers[0][1])
        copy.wait_recv()
        copy.wait_send()

    load_t.wait()
    hi, lo = split(feats[0] * (LOG2E / (TEACHER_TEMP / STUDENT_TEMP)))
    thh[:, 0:width] = hi
    thh[:, width : 2 * width] = hi
    tl[...] = lo

    @pl.loop(0, tiles)
    def _(j):
        load_p(j).wait()
        ph, plo = split(q[j, 0:width, :] * (1.0 / STUDENT_TEMP))
        phl[j, 0:width, :] = ph
        phl[j, width : 2 * width, :] = plo
        scores = mm(thh[...], phl[j]) + mm(tl[...], phl[j, 0:width, :])
        top = jnp.max(scores, axis=0, keepdims=True)
        ex = jnp.exp2(scores - top)
        e[j] = ex
        total = jnp.sum(ex, axis=0, keepdims=True)
        for i in range(per):
            cola[pl.ds(per * j + i, 1), :] = top[:, LANES * i : LANES * (i + 1)]
            cola[pl.ds(per * (tiles + j) + i, 1), :] = total[:, LANES * i : LANES * (i + 1)]

    pl.semaphore_wait(barrier, len(smp_peers) + len(row_peers))

    def student(first, last):
        @pl.loop(first, last)
        def _(j):
            scores = mm(shh[...], phl[j]) + mm(sl[...], phl[j, 0:width, :])
            q[j] = scores
            for r in range(blocks):
                rs = slice(LANES * r, LANES * (r + 1))
                m = mx[rs, :]
                for i in range(per):
                    m = jnp.maximum(m, scores[rs, LANES * i : LANES * (i + 1)])
                mx[rs, :] = m

    def student_start():
        load_s.wait()
        sf = feats[1]
        shi, slo = split(sf * LOG2E)
        shh[:, 0:width] = shi
        shh[:, width : 2 * width] = shi
        sl[...] = slo
        mx[...] = jnp.full(mx.shape, -jnp.inf, f32)

    def student_transpose():
        keep = width // SN
        ht, lt = split((feats[1] * (1.0 / STUDENT_TEMP)).T)
        for core in range(2):
            for chip in range(XN):
                to = (core * XN + chip) * keep
                fr = (2 * chip + core) * keep
                st[0, to : to + keep, :] = ht[fr : fr + keep, :]
                st[1, to : to + keep, :] = lt[fr : fr + keep, :]

    def to_rows(ref, reduce, out, base):
        for r in range(blocks):
            rs = slice(LANES * r, LANES * (r + 1))
            out[base + r : base + r + 1, :] = reduce(ref[rs, :].T, axis=0, keepdims=True)

    def to_columns(v, out):
        for r in range(blocks):
            rs = slice(LANES * r, LANES * (r + 1))
            out[rs, :] = jnp.broadcast_to(v[r : r + 1, :], (LANES, LANES)).T

    def student_totals():
        to_rows(mx, jnp.max, stat, 0)
        to_columns(stat[0:blocks, :], ab)
        mx[...] = jnp.zeros(mx.shape, f32)

        @pl.loop(0, tiles)
        def _(j):
            for r in range(blocks):
                rs = slice(LANES * r, LANES * (r + 1))
                m = ab[rs, :]
                a = mx[rs, :]
                for i in range(per):
                    ls = slice(LANES * i, LANES * (i + 1))
                    v = jnp.exp2(q[j, rs, ls] - m)
                    q[j, rs, ls] = v
                    a = a + v
                mx[rs, :] = a

        to_rows(mx, jnp.sum, stat, blocks)

    def row_pass(it):
        acc[...] = jnp.zeros(acc.shape, f32)

        @pl.loop(0, tiles)
        def _(j):
            ws = [pscale[pl.ds(per * j + i, 1), :] for i in range(per)]
            fs = [peakf[pl.ds(per * j + i, 1), :] for i in range(per)] if it == 0 else None
            for r in range(blocks):
                rs = slice(LANES * r, LANES * (r + 1))
                a = acc[rs, :]
                for i in range(per):
                    ls = slice(LANES * i, LANES * (i + 1))
                    v = e[j, rs, ls]
                    if it == 0:
                        v = v * fs[i]
                        e[j, rs, ls] = v
                    a = a + v * ws[i]
                acc[rs, :] = a

        to_rows(acc, jnp.sum, rowm.at[it], 0)

    def row_start(it):
        row_in[it, pl.ds(p, 1)] = rowm[it : it + 1]
        group_send(lambda k: rowm.at[it], row_in.at[it], row_group, rs_sem.at[it], rr_sem.at[it])

    def row_end(it):
        group_wait(row_in.at[it], row_group, rs_sem.at[it], rr_sem.at[it])
        mass = sum(row_in[it, k] for k in range(PN))
        to_columns(1.0 / mass, cb)

    def col_pass(it):
        @pl.loop(0, tiles)
        def _(j):
            for i in range(per):
                ls = slice(LANES * i, LANES * (i + 1))
                v = jnp.sum(e[j, :, ls] * cb[...], axis=0, keepdims=True)
                col[it, pl.ds(per * j + i, 1), :] = v

    def col_start(it):
        col_in[it, pl.ds(s, 1)] = col[it : it + 1]
        group_send(lambda k: col.at[it], col_in.at[it], smp_group, cs_sem.at[it + 1], cr_sem.at[it + 1])

    def col_end(it):
        group_wait(col_in.at[it], smp_group, cs_sem.at[it + 1], cr_sem.at[it + 1])
        pscale[...] = 1.0 / sum(col_in[it, k] for k in range(SN))

    keep = width // SN
    hk = keep // 2
    mine = pl.multiple_of(c * (width // 2), width // 2)
    other = pl.multiple_of((1 - c) * (width // 2), width // 2)
    across = pl.multiple_of(((x + 2) % XN) * keep, keep)
    ahead = pl.multiple_of(((x + 1) % XN) * keep, keep)
    behind = pl.multiple_of(((x + XN - 1) % XN) * keep, keep)
    here = pl.multiple_of(x * keep, keep)

    def core_copy(t):
        return rc(e.at[t, pl.ds(other, width // 2)], cr.at[t], ks_sem.at[t], kr_sem.at[t], sibling)

    def x_copy(t, k):
        row, dst, dev = [
            (across, xa.at[t, 0], right),
            (across + hk, xa.at[t, 1], left),
            (ahead + hk, xb.at[t, 0, pl.ds(hk, hk)], right),
            (behind, xb.at[t, 1, pl.ds(0, hk)], left),
            (ahead, xb.at[t, 0, pl.ds(0, hk)], right),
            (behind + hk, xb.at[t, 1, pl.ds(hk, hk)], left),
        ][k]
        src = cr.at[t, pl.ds(pl.multiple_of(row, 8), hk)]
        return rc(src, dst, xs_sem.at[t, k], xr_sem.at[t, k], dev)

    def out_copy(t):
        cols = pl.ds(pl.multiple_of(t * TILE, TILE), TILE)
        return pltpu.make_async_copy(gpo.at[t], gp_out.at[:, cols], out_sem.at[t])

    def gp_terms(t):
        d = dh[t]
        e[t, 0:width, :] = mm(st[0], d) + mm(st[1], d) + mm(st[0], dl[t])
        core_copy(t).start()

    def gp_core(t):
        core_copy(t).wait_recv()
        cr[t] = cr[t] + e[t, pl.ds(mine, width // 2), :]
        x_copy(t, 0).start()
        x_copy(t, 1).start()

    def gp_relay(t):
        x_copy(t, 0).wait_recv()
        x_copy(t, 1).wait_recv()
        a = pl.ds(pl.multiple_of(ahead, 8), hk)
        cr[t, a, :] = cr[t, a, :] + xa[t, 0]
        b = pl.ds(pl.multiple_of(behind + hk, 8), hk)
        cr[t, b, :] = cr[t, b, :] + xa[t, 1]
        for k in range(2, 6):
            x_copy(t, k).start()

    def gp_end(t):
        for k in range(2, 6):
            x_copy(t, k).wait_recv()
        gpo[t] = cr[t, pl.ds(here, keep), :] + xb[t, 0] + xb[t, 1]
        out_copy(t).start()
        core_copy(t).wait_send()
        for k in range(6):
            x_copy(t, k).wait_send()

    part = rows // 2
    chunk = part // YN
    hc = chunk // 2
    piece = chunk // ZN

    def chunk_at(r, d, low, size):
        return pl.ds(pl.multiple_of((r % 2) * part + ((y + d) % YN) * chunk + low, 8), size)

    def y_copy(r, k):
        d, low, dst, dev = [
            (2, 0, gya.at[r, 0], y_right),
            (2, hc, gya.at[r, 1], y_left),
            (1, hc, gyb.at[r, 0, pl.ds(hc, hc)], y_right),
            (YN - 1, 0, gyb.at[r, 1, pl.ds(0, hc)], y_left),
            (1, 0, gyb.at[r, 0, pl.ds(0, hc)], y_right),
            (YN - 1, hc, gyb.at[r, 1, pl.ds(hc, hc)], y_left),
        ][k]
        return rc(gfs.at[r // 2, chunk_at(r, d, low, hc)], dst, ys_sem.at[r, k], yr_sem.at[r, k], dev)

    def y_gather(r, k):
        d, low, size, dev = [
            (0, 0, chunk, y_right),
            (0, 0, chunk, y_left),
            (YN - 1, 0, hc, y_right),
            (1, hc, hc, y_left),
        ][k]
        src = gfo.at[chunk_at(r, d, low, size)]
        return rc(src, src, ys_sem.at[r, 6 + k], yr_sem.at[r, 6 + k], dev)

    def y_arrive(r, k):
        d, low, size = [(YN - 1, 0, chunk), (1, 0, chunk), (2, 0, hc), (2, hc, hc)][k]
        dst = gfo.at[chunk_at(r, d, low, size)]
        rc(dst, dst, ys_sem.at[r, 6 + k], yr_sem.at[r, 6 + k], y_right).wait_recv()

    def gf_a(r):
        for k in range(4):
            y_copy(r, k).start()

    def gf_b(r):
        for k in range(2):
            y_copy(r, k).wait_recv()
        a = chunk_at(r, 1, 0, hc)
        gfs[r // 2, a, :] = gfs[r // 2, a, :] + gya[r, 0]
        b = chunk_at(r, YN - 1, hc, hc)
        gfs[r // 2, b, :] = gfs[r // 2, b, :] + gya[r, 1]
        y_copy(r, 4).start()
        y_copy(r, 5).start()

    def gf_c(r):
        for k in range(2, 6):
            y_copy(r, k).wait_recv()
        for k in range(ZN):
            rs = slice(k * piece, (k + 1) * piece)
            own = gfs[r // 2, chunk_at(r, 0, k * piece, piece), :]
            gft[r, k] = own + gyb[r, 0, rs, :] + gyb[r, 1, rs, :]
        group_send(lambda k: gft.at[r, k], gfz.at[r], z_group, zs_sem.at[r], zr_sem.at[r])

    def gf_d(r):
        group_wait(gfz.at[r], z_group, zs_sem.at[r], zr_sem.at[r])
        gfz[r, pl.ds(z, 1)] = gft[r, pl.ds(z, 1)]
        if r < 2:
            targets = sum(gfz[r, k] for k in range(ZN))
            probs = sum(gfz[r + 2, k] for k in range(ZN))
            scale = cb[chunk_at(r, 0, z * piece, piece), :]
            scale = jnp.concatenate([scale] * (width // LANES), axis=1)
            gfz2[r, pl.ds(z, 1)] = (probs - scale * targets)[None]
            group_send(lambda k: gfz2.at[r, z], gfz2.at[r], z_group, zs_sem.at[4 + r], zr_sem.at[4 + r])

    def gf_e(r):
        group_wait(gfz2.at[r], z_group, zs_sem.at[4 + r], zr_sem.at[4 + r])
        for k in range(ZN):
            gfo[chunk_at(r, 0, k * piece, piece), :] = gfz2[r, k]
        y_gather(r, 0).start()
        y_gather(r, 1).start()

    def gf_f(r):
        y_arrive(r, 0)
        y_arrive(r, 1)
        y_gather(r, 2).start()
        y_gather(r, 3).start()

    def gf_copy(r):
        rs = pl.ds(r * part, part)
        return pltpu.make_async_copy(gfo.at[rs], gf_out.at[rs], out_sem.at[tiles + r])

    def gf_g(r):
        y_arrive(r, 2)
        y_arrive(r, 3)
        gf_copy(r).start()
        for k in range(6):
            y_copy(r, k).wait_send()
            y_copy(r + 2, k).wait_send()
        for k in range(4):
            y_gather(r, k).wait_send()

    def feat_terms(j, which, rs):
        gfacc[which, rs, :] += mm_t(dh[j, rs, :], phl[j])
        gfacc[which, rs, 0:width] += mm_t(dl[j, rs, :], phl[j, 0:width, :])

    everything = slice(0, rows)
    halves = [slice(0, part), slice(part, rows)]

    def probs_terms():
        gfacc[...] = jnp.zeros(gfacc.shape, f32)

        @pl.loop(0, tiles)
        def _(j):
            hi, lo = split(q[j])
            dh[j] = hi
            dl[j] = lo
            feat_terms(j, 1, everything)

    def probs_sum():
        for k in range(width // LANES):
            ls = slice(LANES * k, LANES * (k + 1))
            us = slice(width + LANES * k, width + LANES * (k + 1))
            gfs[1, :, ls] = (gfacc[1, :, ls] + gfacc[1, :, us]) * ab[...]
        gf_a(2)
        gf_a(3)

    def mass_terms(h):
        @pl.loop(0, tiles)
        def _(j):
            if h == 0:
                for k in range(per):
                    ls = slice(LANES * k, LANES * (k + 1))
                    hi, lo = split(e[j, :, ls] * pscale[pl.ds(per * j + k, 1), :])
                    dh[j, :, ls] = hi
                    dl[j, :, ls] = lo
            feat_terms(j, 0, halves[h])

        rs = halves[h]
        gfs[0, rs, :] = gfacc[0, rs, 0:width] + gfacc[0, rs, width : 2 * width]
        gf_a(h)

    half = per * tiles
    cola_in[pl.ds(s, 1)] = cola[...][None]
    group_send(lambda k: cola, cola_in, smp_group, cs_sem.at[0], cr_sem.at[0])
    student_start()
    student(0, tiles // 2)
    group_wait(cola_in, smp_group, cs_sem.at[0], cr_sem.at[0])
    tops = [cola_in[k, 0:half, :] for k in range(SN)]
    top = functools.reduce(jnp.maximum, tops)
    pscale[...] = 1.0 / sum(cola_in[k, half : 2 * half, :] * jnp.exp2(tops[k] - top) for k in range(SN))
    peakf[...] = jnp.exp2(cola[0:half, :] - top)

    row_pass(0)
    row_start(0)
    student(tiles // 2, tiles)
    student_totals()
    row_end(0)
    col_pass(0)
    col_start(0)
    stat_in[pl.ds(p, 1)] = stat[...][None]
    group_send(lambda k: stat, stat_in, row_group, st_sem.at[0], st_sem.at[1])
    student_transpose()
    col_end(0)

    row_pass(1)
    row_start(1)
    probs_terms()
    group_wait(stat_in, row_group, st_sem.at[0], st_sem.at[1])
    tops = [stat_in[k, 0:blocks, :] for k in range(PN)]
    top = functools.reduce(jnp.maximum, tops)
    total = sum(stat_in[k, blocks : 2 * blocks, :] * jnp.exp2(tops[k] - top) for k in range(PN))
    to_columns(jnp.exp2(stat[0:blocks, :] - top) / total, ab)
    row_end(1)
    col_pass(1)
    col_start(1)
    probs_sum()
    col_end(1)

    row_pass(2)
    row_start(2)
    gf_b(2)
    gf_b(3)
    mass_terms(0)
    mass_terms(1)
    row_end(2)

    lag_core, lag_relay, lag_end = 2, 6, 10
    at = {
        0: [(gf_c, 2), (gf_c, 3), (gf_b, 0)],
        3: [(gf_b, 1)],
        4: [(gf_c, 0)],
        6: [(gf_c, 1)],
        8: [(gf_d, 2), (gf_d, 3)],
        9: [(gf_d, 0)],
        10: [(gf_d, 1)],
        12: [(gf_e, 0)],
        13: [(gf_e, 1)],
        14: [(gf_f, 0)],
        15: [(gf_f, 1)],
        16: [(gf_g, 0)],
        17: [(gf_g, 1)],
    }

    @pl.loop(0, tiles + lag_end)
    def _(i):
        @pl.when(i < tiles)
        def _():
            for k in range(per):
                ls = slice(LANES * k, LANES * (k + 1))
                w = pscale[pl.ds(per * i + k, 1), :]
                d = q[i, :, ls] * ab[...] - (cb[...] * e[i, :, ls]) * w
                dhi, dlo = split(d)
                dh[i, :, ls] = dhi
                dl[i, :, ls] = dlo
            gp_terms(i)

        @pl.when((i >= lag_core) & (i < tiles + lag_core))
        def _():
            gp_core(i - lag_core)

        @pl.when((i >= lag_relay) & (i < tiles + lag_relay))
        def _():
            gp_relay(i - lag_relay)

        for when, todo in at.items():

            @pl.when(i == when)
            def _(todo=todo):
                for f, h in todo:
                    f(h)

        @pl.when(i >= lag_end)
        def _():
            gp_end(i - lag_end)

    for t in range(tiles):
        out_copy(t).wait()
    for h in range(2):
        gf_copy(h).wait()


def finish(gf_in, gp_in, gf_out, gp_out, gf_mid, gp_mid, sem):
    copies = []
    for k, (src, mid, dst) in enumerate(((gf_in, gf_mid, gf_out), (gp_in, gp_mid, gp_out))):
        n = src.shape[0] // 2
        for h in range(2):
            rs = pl.ds(h * n, n)
            first = pltpu.make_async_copy(src.at[rs], mid.at[rs], sem.at[0, 2 * k + h])
            second = pltpu.make_async_copy(mid.at[rs], dst.at[rs], sem.at[1, 2 * k + h])
            first.start()
            copies.append((first, second))
    for first, second in copies:
        first.wait()
        second.start()
    for first, second in copies:
        second.wait()


def local(SN, PN, teacher_feats, student_feats, prototypes):
    rows, width = teacher_feats.shape
    protos = prototypes.shape[1]
    tiles = protos // TILE
    half = protos // LANES
    blocks = rows // LANES
    ZN = PN // YN
    chunk = rows // 2 // YN
    piece = chunk // ZN
    V = pltpu.VMEM
    DMA = pltpu.SemaphoreType.DMA
    scratch = [
        V((2, rows, width), f32),
        V((rows, 2 * width), bf16),
        V((rows, width), bf16),
        V((rows, 2 * width), bf16),
        V((rows, width), bf16),
        V((2, width, rows), bf16),
        V((tiles, 2 * width, TILE), bf16),
        V((tiles, rows, TILE), f32),
        V((tiles, rows, TILE), f32),
        V((tiles, rows, TILE), bf16),
        V((tiles, rows, TILE), bf16),
        V((2 * half, LANES), f32),
        V((SN, 2 * half, LANES), f32),
        V((ITERS - 1, half, LANES), f32),
        V((ITERS - 1, SN, half, LANES), f32),
        V((half, LANES), f32),
        V((half, LANES), f32),
        V((rows, LANES), f32),
        V((rows, LANES), f32),
        V((rows, LANES), f32),
        V((rows, LANES), f32),
        V((ITERS, blocks, LANES), f32),
        V((ITERS, PN, blocks, LANES), f32),
        V((2 * blocks, LANES), f32),
        V((PN, 2 * blocks, LANES), f32),
        V((2, rows, 2 * width), f32),
        V((2, rows, width), f32),
        V((4, 2, chunk // 2, width), f32),
        V((4, 2, chunk, width), f32),
        V((4, ZN, piece, width), f32),
        V((4, ZN, piece, width), f32),
        V((2, ZN, piece, width), f32),
        V((rows, width), f32),
        V((tiles, width // 2, TILE), f32),
        V((tiles, 2, width // SN // 2, TILE), f32),
        V((tiles, 2, width // SN, TILE), f32),
        V((tiles, width // SN, TILE), f32),
        DMA((2 + tiles,)),
        DMA((ITERS,)),
        DMA((ITERS,)),
        DMA((ITERS,)),
        DMA((ITERS,)),
        DMA((2,)),
        DMA((4, 10)),
        DMA((4, 10)),
        DMA((6,)),
        DMA((6,)),
        DMA((tiles,)),
        DMA((tiles,)),
        DMA((tiles, 6)),
        DMA((tiles, 6)),
        DMA((tiles + 2,)),
    ]
    flops = 2 * rows * width * protos
    shapes = (
        jax.ShapeDtypeStruct((rows, width), f32),
        jax.ShapeDtypeStruct((width // SN, protos), f32),
    )
    outs = pl.pallas_call(
        functools.partial(kernel, SN, PN),
        out_shape=shapes,
        in_specs=[pl.BlockSpec(memory_space=pl.ANY)] * 3,
        out_specs=(pl.BlockSpec(memory_space=pl.ANY),) * 2,
        scratch_shapes=scratch,
        compiler_params=pltpu.CompilerParams(
            collective_id=0, has_side_effects=True, vmem_limit_bytes=62 * 1024 * 1024
        ),
        cost_estimate=pl.CostEstimate(
            flops=12 * flops, bytes_accessed=4 * width * (protos + 4 * rows), transcendentals=2 * rows * protos
        ),
    )(teacher_feats, student_feats, prototypes)
    return pl.pallas_call(
        finish,
        out_shape=shapes,
        in_specs=[pl.BlockSpec(memory_space=pl.ANY)] * 2,
        out_specs=(pl.BlockSpec(memory_space=pl.ANY),) * 2,
        scratch_shapes=[V((rows, width), f32), V((width // SN, protos), f32), DMA((2, 4))],
        cost_estimate=pl.CostEstimate(
            flops=0, bytes_accessed=8 * (rows * width + width // SN * protos), transcendentals=0
        ),
    )(*outs)


def solution(mesh):
    SN, PN = mesh.shape["smp"], mesh.shape["proto"]
    in_specs = (P("smp", None), P("smp", None), P(None, "proto"))
    out_specs = (P("smp", None), P("smp", "proto"))
    return jax.shard_map(
        functools.partial(local, SN, PN), mesh=mesh, in_specs=in_specs, out_specs=out_specs, check_vma=False
    )
```

time: 113 us -> 97.7 us (0.86)
  Pallas kernels: 108 us -> 96.9 us
  local copies, waits for them, and re-layouts: 4.13 us -> 0 us
    pallas_call x1 -> x2, Pallas kernels: 108 us -> 96.9 us  [the longest x1 94.7 us: local(): pl.pallas_call(functools.partial(kernel, SN, PN), out_shape=shapes, in_sp...]
    unnamed x2 -> x0, local copies, waits for them, and re-layouts: 4.13 us -> none
where the time goes in v2:
time: 97.7 us; the launch traced here: 97.6 us
  Pallas kernels  96.9 us (99%)
    pallas_call x1, Pallas kernels, local(): pl.pallas_call(functools.partial(kernel, SN, PN), out_shape=shapes, in_sp...  94.7 us
    pallas_call x1, Pallas kernels, local(): pl.pallas_call(finish, out_shape=shapes, in_specs=[pl.BlockSpec(memory_sp...  2.2 us

profile of v2, /device:TPU:1, one launch (start us, length us, event | category | flops | bytes accessed | tf_op | source)
XLA Modules:
  0.0 97.6 jit_solution(1961145024928005287)
XLA Ops:
  0.6 94.7 %shard_map.50 = (f32[512,384]{1,0:T(8,128)}, f32[48,4096]{1,0:T(8,128)}) custom-call(f32[512,384]{1,0:T(8,128)} %t_hbm.1, f32[512,384]{1,0:T(8,128)} %s_hbm.1, f32[384,4096]{1,0:T(8,128)} %p_hbm.1), custom_call_target="tpu_custom_call" | custom-call | flops 19327352832 | bytes 9437184 | tf_op jit(solution)/shard_map/pallas_call | solution.py:672
  95.4 2.2 %shard_map.51 = (f32[512,384]{1,0:T(8,128)}, f32[48,4096]{1,0:T(8,128)}) custom-call(f32[512,384]{1,0:T(8,128)} %get-tuple-element.4.gf_in, f32[48,4096]{1,0:T(8,128)} %get-tuple-element.5.gp_in), custom_call_target="tpu_custom_call" | custom-call | bytes 3145728 | tf_op jit(solution)/shard_map/pallas_call | solution.py:685

commit v3 on v2

--- a/solution.py
+++ b/solution.py
@@ -328,6 +328,11 @@
         x_copy(t, 0).start()
         x_copy(t, 1).start()
 
+        @pl.when(t < 2)
+        def _():
+            x_copy(t, 2).start()
+            x_copy(t, 3).start()
+
     def gp_relay(t):
         x_copy(t, 0).wait_recv()
         x_copy(t, 1).wait_recv()
@@ -335,8 +340,14 @@
         cr[t, a, :] = cr[t, a, :] + xa[t, 0]
         b = pl.ds(pl.multiple_of(behind + hk, 8), hk)
         cr[t, b, :] = cr[t, b, :] + xa[t, 1]
-        for k in range(2, 6):
-            x_copy(t, k).start()
+
+        @pl.when(t >= 2)
+        def _():
+            x_copy(t, 2).start()
+            x_copy(t, 3).start()
+
+        x_copy(t, 4).start()
+        x_copy(t, 5).start()
 
     def gp_end(t):
         for k in range(2, 6):
@@ -449,10 +460,8 @@
     everything = slice(0, rows)
     halves = [slice(0, part), slice(part, rows)]
 
-    def probs_terms():
-        gfacc[...] = jnp.zeros(gfacc.shape, f32)
-
-        @pl.loop(0, tiles)
+    def probs_terms(first, last):
+        @pl.loop(first, last)
         def _(j):
             hi, lo = split(q[j])
             dh[j] = hi
@@ -467,8 +476,8 @@
         gf_a(2)
         gf_a(3)
 
-    def mass_terms(h):
-        @pl.loop(0, tiles)
+    def mass_terms(h, first, last):
+        @pl.loop(first, last)
         def _(j):
             if h == 0:
                 for k in range(per):
@@ -478,6 +487,7 @@
                     dl[j, :, ls] = lo
             feat_terms(j, 0, halves[h])
 
+    def mass_sum(h):
         rs = halves[h]
         gfs[0, rs, :] = gfacc[0, rs, 0:width] + gfacc[0, rs, width : 2 * width]
         gf_a(h)
@@ -486,7 +496,8 @@
     cola_in[pl.ds(s, 1)] = cola[...][None]
     group_send(lambda k: cola, cola_in, smp_group, cs_sem.at[0], cr_sem.at[0])
     student_start()
-    student(0, tiles // 2)
+    student(0, 5)
+    gfacc[...] = jnp.zeros(gfacc.shape, f32)
     group_wait(cola_in, smp_group, cs_sem.at[0], cr_sem.at[0])
     tops = [cola_in[k, 0:half, :] for k in range(SN)]
     top = functools.reduce(jnp.maximum, tops)
@@ -495,19 +506,19 @@
 
     row_pass(0)
     row_start(0)
-    student(tiles // 2, tiles)
+    student(5, tiles)
     student_totals()
     row_end(0)
     col_pass(0)
     col_start(0)
     stat_in[pl.ds(p, 1)] = stat[...][None]
     group_send(lambda k: stat, stat_in, row_group, st_sem.at[0], st_sem.at[1])
-    student_transpose()
+    probs_terms(0, 4)
     col_end(0)
 
     row_pass(1)
     row_start(1)
-    probs_terms()
+    probs_terms(4, tiles)
     group_wait(stat_in, row_group, st_sem.at[0], st_sem.at[1])
     tops = [stat_in[k, 0:blocks, :] for k in range(PN)]
     top = functools.reduce(jnp.maximum, tops)
@@ -517,25 +528,27 @@
     col_pass(1)
     col_start(1)
     probs_sum()
+    student_transpose()
     col_end(1)
 
     row_pass(2)
     row_start(2)
     gf_b(2)
     gf_b(3)
-    mass_terms(0)
-    mass_terms(1)
+    mass_terms(0, 0, tiles)
+    mass_sum(0)
+    mass_terms(1, 0, 2)
     row_end(2)
 
     lag_core, lag_relay, lag_end = 2, 6, 10
     at = {
-        0: [(gf_c, 2), (gf_c, 3), (gf_b, 0)],
-        3: [(gf_b, 1)],
-        4: [(gf_c, 0)],
-        6: [(gf_c, 1)],
-        8: [(gf_d, 2), (gf_d, 3)],
+        2: [(gf_c, 2), (gf_c, 3)],
+        3: [(gf_c, 0)],
+        4: [(gf_b, 1)],
+        7: [(gf_d, 2), (gf_d, 3)],
+        8: [(gf_c, 1)],
         9: [(gf_d, 0)],
-        10: [(gf_d, 1)],
+        11: [(gf_d, 1)],
         12: [(gf_e, 0)],
         13: [(gf_e, 1)],
         14: [(gf_f, 0)],
@@ -544,20 +557,35 @@
         17: [(gf_g, 1)],
     }
 
-    @pl.loop(0, tiles + lag_end)
+    def dlogits(i):
+        for k in range(per):
+            ls = slice(LANES * k, LANES * (k + 1))
+            w = pscale[pl.ds(per * i + k, 1), :]
+            d = q[i, :, ls] * ab[...] - (cb[...] * e[i, :, ls]) * w
+            dhi, dlo = split(d)
+            dh[i, :, ls] = dhi
+            dl[i, :, ls] = dlo
+
+    @pl.loop(0, 2)
+    def _(i):
+        dlogits(i)
+        gp_terms(i)
+
+    mass_terms(1, 2, 5)
+    gf_b(0)
+    gp_core(0)
+    mass_terms(1, 5, tiles)
+    mass_sum(1)
+    gp_core(1)
+
+    @pl.loop(2, tiles + lag_end)
     def _(i):
         @pl.when(i < tiles)
         def _():
-            for k in range(per):
-                ls = slice(LANES * k, LANES * (k + 1))
-                w = pscale[pl.ds(per * i + k, 1), :]
-                d = q[i, :, ls] * ab[...] - (cb[...] * e[i, :, ls]) * w
-                dhi, dlo = split(d)
-                dh[i, :, ls] = dhi
-                dl[i, :, ls] = dlo
+            dlogits(i)
             gp_terms(i)
 
-        @pl.when((i >= lag_core) & (i < tiles + lag_core))
+        @pl.when((i >= 2 + lag_core) & (i < tiles + lag_core))
         def _():
             gp_core(i - lag_core)
 

time: 97.7 us -> 92.1 us (0.943)
  Pallas kernels: 96.9 us -> 91.3 us
    pallas_call x1, Pallas kernels: 94.7 us -> 89.1 us  [local(): pl.pallas_call(functools.partial(kernel, SN, PN), out_shape=shapes, in_sp...]
where the time goes in v3:
time: 92.1 us; the launch traced here: 91.9 us
  Pallas kernels  91.3 us (99%)
    pallas_call x1, Pallas kernels, local(): pl.pallas_call(functools.partial(kernel, SN, PN), out_shape=shapes, in_sp...  89.1 us
    pallas_call x1, Pallas kernels, local(): pl.pallas_call(finish, out_shape=shapes, in_specs=[pl.BlockSpec(memory_sp...  2.2 us

profile of v3, /device:TPU:1, one launch (start us, length us, event | category | flops | bytes accessed | tf_op | source)
XLA Modules:
  0.0 91.9 jit_solution(14635168621152880107)
XLA Ops:
  0.6 89.1 %shard_map.50 = (f32[512,384]{1,0:T(8,128)}, f32[48,4096]{1,0:T(8,128)}) custom-call(f32[512,384]{1,0:T(8,128)} %t_hbm.1, f32[512,384]{1,0:T(8,128)} %s_hbm.1, f32[384,4096]{1,0:T(8,128)} %p_hbm.1), custom_call_target="tpu_custom_call" | custom-call | flops 19327352832 | bytes 9437184 | tf_op jit(solution)/shard_map/pallas_call | solution.py:700
  89.7 2.2 %shard_map.51 = (f32[512,384]{1,0:T(8,128)}, f32[48,4096]{1,0:T(8,128)}) custom-call(f32[512,384]{1,0:T(8,128)} %get-tuple-element.4.gf_in, f32[48,4096]{1,0:T(8,128)} %get-tuple-element.5.gp_in), custom_call_target="tpu_custom_call" | custom-call | bytes 3145728 | tf_op jit(solution)/shard_map/pallas_call | solution.py:713

commit v4 on v3

--- a/solution.py
+++ b/solution.py
@@ -77,7 +77,6 @@
     cr,
     xa,
     xb,
-    gpo,
     load_sem,
     cs_sem,
     cr_sem,
@@ -92,7 +91,6 @@
     kr_sem,
     xs_sem,
     xr_sem,
-    out_sem,
 ):
     ZN = PN // YN
     XN = SN // 2
@@ -313,10 +311,6 @@
         src = cr.at[t, pl.ds(pl.multiple_of(row, 8), hk)]
         return rc(src, dst, xs_sem.at[t, k], xr_sem.at[t, k], dev)
 
-    def out_copy(t):
-        cols = pl.ds(pl.multiple_of(t * TILE, TILE), TILE)
-        return pltpu.make_async_copy(gpo.at[t], gp_out.at[:, cols], out_sem.at[t])
-
     def gp_terms(t):
         d = dh[t]
         e[t, 0:width, :] = mm(st[0], d) + mm(st[1], d) + mm(st[0], dl[t])
@@ -352,8 +346,8 @@
     def gp_end(t):
         for k in range(2, 6):
             x_copy(t, k).wait_recv()
-        gpo[t] = cr[t, pl.ds(here, keep), :] + xb[t, 0] + xb[t, 1]
-        out_copy(t).start()
+        cols = pl.ds(pl.multiple_of(t * TILE, TILE), TILE)
+        gp_out[:, cols] = cr[t, pl.ds(here, keep), :] + xb[t, 0] + xb[t, 1]
         core_copy(t).wait_send()
         for k in range(6):
             x_copy(t, k).wait_send()
@@ -439,14 +433,11 @@
         y_gather(r, 2).start()
         y_gather(r, 3).start()
 
-    def gf_copy(r):
-        rs = pl.ds(r * part, part)
-        return pltpu.make_async_copy(gfo.at[rs], gf_out.at[rs], out_sem.at[tiles + r])
-
     def gf_g(r):
         y_arrive(r, 2)
         y_arrive(r, 3)
-        gf_copy(r).start()
+        rs = pl.ds(r * part, part)
+        gf_out[rs, :] = gfo[rs, :]
         for k in range(6):
             y_copy(r, k).wait_send()
             y_copy(r + 2, k).wait_send()
@@ -485,7 +476,7 @@
                     hi, lo = split(e[j, :, ls] * pscale[pl.ds(per * j + k, 1), :])
                     dh[j, :, ls] = hi
                     dl[j, :, ls] = lo
-            feat_terms(j, 0, halves[h])
+            feat_terms(j, 0, everything)
 
     def mass_sum(h):
         rs = halves[h]
@@ -537,16 +528,16 @@
     gf_b(3)
     mass_terms(0, 0, tiles)
     mass_sum(0)
-    mass_terms(1, 0, 2)
+    mass_sum(1)
     row_end(2)
 
     lag_core, lag_relay, lag_end = 2, 6, 10
     at = {
         2: [(gf_c, 2), (gf_c, 3)],
-        3: [(gf_c, 0)],
-        4: [(gf_b, 1)],
-        7: [(gf_d, 2), (gf_d, 3)],
-        8: [(gf_c, 1)],
+        4: [(gf_c, 0)],
+        3: [(gf_b, 1)],
+        6: [(gf_d, 2), (gf_d, 3)],
+        5: [(gf_c, 1)],
         9: [(gf_d, 0)],
         11: [(gf_d, 1)],
         12: [(gf_e, 0)],
@@ -571,12 +562,7 @@
         dlogits(i)
         gp_terms(i)
 
-    mass_terms(1, 2, 5)
     gf_b(0)
-    gp_core(0)
-    mass_terms(1, 5, tiles)
-    mass_sum(1)
-    gp_core(1)
 
     @pl.loop(2, tiles + lag_end)
     def _(i):
@@ -585,7 +571,7 @@
             dlogits(i)
             gp_terms(i)
 
-        @pl.when((i >= 2 + lag_core) & (i < tiles + lag_core))
+        @pl.when((i >= lag_core) & (i < tiles + lag_core))
         def _():
             gp_core(i - lag_core)
 
@@ -604,27 +590,18 @@
         def _():
             gp_end(i - lag_end)
 
-    for t in range(tiles):
-        out_copy(t).wait()
-    for h in range(2):
-        gf_copy(h).wait()
-
-
-def finish(gf_in, gp_in, gf_out, gp_out, gf_mid, gp_mid, sem):
+
+def finish(gf_in, gp_in, gf_out, gp_out, sem):
     copies = []
-    for k, (src, mid, dst) in enumerate(((gf_in, gf_mid, gf_out), (gp_in, gp_mid, gp_out))):
+    for k, (src, dst) in enumerate(((gf_in, gf_out), (gp_in, gp_out))):
         n = src.shape[0] // 2
         for h in range(2):
             rs = pl.ds(h * n, n)
-            first = pltpu.make_async_copy(src.at[rs], mid.at[rs], sem.at[0, 2 * k + h])
-            second = pltpu.make_async_copy(mid.at[rs], dst.at[rs], sem.at[1, 2 * k + h])
-            first.start()
-            copies.append((first, second))
-    for first, second in copies:
-        first.wait()
-        second.start()
-    for first, second in copies:
-        second.wait()
+            copies.append(pltpu.make_async_copy(src.at[rs], dst.at[rs], sem.at[2 * k + h]))
+    for copy in copies:
+        copy.start()
+    for copy in copies:
+        copy.wait()
 
 
 def local(SN, PN, teacher_feats, student_feats, prototypes):
@@ -675,7 +652,6 @@
         V((tiles, width // 2, TILE), f32),
         V((tiles, 2, width // SN // 2, TILE), f32),
         V((tiles, 2, width // SN, TILE), f32),
-        V((tiles, width // SN, TILE), f32),
         DMA((2 + tiles,)),
         DMA((ITERS,)),
         DMA((ITERS,)),
@@ -690,7 +666,6 @@
         DMA((tiles,)),
         DMA((tiles, 6)),
         DMA((tiles, 6)),
-        DMA((tiles + 2,)),
     ]
     flops = 2 * rows * width * protos
     shapes = (
@@ -699,12 +674,12 @@
     )
     outs = pl.pallas_call(
         functools.partial(kernel, SN, PN),
-        out_shape=shapes,
+        out_shape=tuple(V(o.shape, o.dtype) for o in shapes),
         in_specs=[pl.BlockSpec(memory_space=pl.ANY)] * 3,
-        out_specs=(pl.BlockSpec(memory_space=pl.ANY),) * 2,
+        out_specs=(pl.BlockSpec(memory_space=pltpu.VMEM),) * 2,
         scratch_shapes=scratch,
         compiler_params=pltpu.CompilerParams(
-            collective_id=0, has_side_effects=True, vmem_limit_bytes=62 * 1024 * 1024
+            collective_id=0, has_side_effects=True, vmem_limit_bytes=60 * 1024 * 1024
         ),
         cost_estimate=pl.CostEstimate(
             flops=12 * flops, bytes_accessed=4 * width * (protos + 4 * rows), transcendentals=2 * rows * protos
@@ -713,9 +688,10 @@
     return pl.pallas_call(
         finish,
         out_shape=shapes,
-        in_specs=[pl.BlockSpec(memory_space=pl.ANY)] * 2,
+        in_specs=[pl.BlockSpec(memory_space=pltpu.VMEM)] * 2,
         out_specs=(pl.BlockSpec(memory_space=pl.ANY),) * 2,
-        scratch_shapes=[V((rows, width), f32), V((width // SN, protos), f32), DMA((2, 4))],
+        scratch_shapes=[DMA((4,))],
+        compiler_params=pltpu.CompilerParams(vmem_limit_bytes=4 * 1024 * 1024),
         cost_estimate=pl.CostEstimate(
             flops=0, bytes_accessed=8 * (rows * width + width // SN * protos), transcendentals=0
         ),

time: 92.1 us -> 89 us (0.966)
  Pallas kernels: 91.3 us -> 88.3 us
    pallas_call x1, Pallas kernels: 89.1 us -> 87.2 us  [local(): pl.pallas_call(functools.partial(kernel, SN, PN), out_shape=tuple((V(o.sh...]
    pallas_call x1, Pallas kernels: 2.2 us -> 1.17 us  [local(): pl.pallas_call(finish, out_shape=shapes, in_specs=[pl.BlockSpec(memory_sp...]
where the time goes in v4:
time: 89 us
  Pallas kernels  88.3 us (99%)
    pallas_call x1, Pallas kernels, local(): pl.pallas_call(functools.partial(kernel, SN, PN), out_shape=tuple((V(o.sh...  87.2 us

profile of v4, /device:TPU:1, one launch (start us, length us, event | category | flops | bytes accessed | tf_op | source)
XLA Modules:
  0.0 89.0 jit_solution(8153402814764824001)
XLA Ops:
  0.6 87.2 %shard_map.50 = (f32[512,384]{1,0:T(8,128)S(1)}, f32[48,4096]{1,0:T(8,128)S(1)}) custom-call(f32[512,384]{1,0:T(8,128)} %t_hbm.1, f32[512,384]{1,0:T(8,128)} %s_hbm.1, f32[384,4096]{1,0:T(8,128)} %p_hbm.1), custom_call_target="tpu_custom_call" | custom-call | flops 19327352832 | bytes 9437184 | tf_op jit(solution)/shard_map/pallas_call | solution.py:675
  87.8 1.2 %shard_map.51 = (f32[512,384]{1,0:T(8,128)}, f32[48,4096]{1,0:T(8,128)}) custom-call(f32[512,384]{1,0:T(8,128)S(1)} %get-tuple-element.4.gf_in, f32[48,4096]{1,0:T(8,128)S(1)} %get-tuple-element.5.gp_in), custom_call_target="tpu_custom_call" | custom-call | bytes 3145728 | tf_op jit(solution)/shard_map/pallas_call | solution.py:688

commit v5 on v4

--- a/solution.py
+++ b/solution.py
@@ -91,6 +91,9 @@
     kr_sem,
     xs_sem,
     xr_sem,
+    enter_sem,
+    wa,
+    wb,
 ):
     ZN = PN // YN
     XN = SN // 2
@@ -127,10 +130,6 @@
             src_ref=src, dst_ref=dst, send_sem=ss, recv_sem=rs, device_id=dev, device_id_type=MESH
         )
 
-    barrier = pltpu.get_barrier_semaphore()
-    for _, dev in smp_group[2] + row_group[2]:
-        pl.semaphore_signal(barrier, inc=1, device_id=dev, device_id_type=MESH)
-
     load_t = pltpu.make_async_copy(t_hbm, feats.at[0], load_sem.at[0])
     load_s = pltpu.make_async_copy(s_hbm, feats.at[1], load_sem.at[1])
 
@@ -144,6 +143,20 @@
     for j in range(tiles):
         load_p(j).start()
     load_s.start()
+
+    barrier = pltpu.get_barrier_semaphore()
+    y_peers = [(s, z * YN + (y + dy) % YN) for dy in range(1, YN)]
+    greet = [dev for _, dev in z_group[2]] + y_peers + [dev for _, dev in smp_group[2]]
+    for dev in greet:
+        pl.semaphore_signal(barrier, inc=1, device_id=dev, device_id_type=MESH)
+
+    def enter_start():
+        pl.semaphore_wait(barrier, len(greet))
+        for dev in y_peers:
+            pl.semaphore_signal(enter_sem, inc=1, device_id=dev, device_id_type=MESH)
+
+    def enter_wait():
+        pl.semaphore_wait(enter_sem, len(y_peers))
 
     def group_send(src, dst, group, ssem, rsem):
         me, n, peers = group
@@ -178,7 +191,7 @@
             cola[pl.ds(per * j + i, 1), :] = top[:, LANES * i : LANES * (i + 1)]
             cola[pl.ds(per * (tiles + j) + i, 1), :] = total[:, LANES * i : LANES * (i + 1)]
 
-    pl.semaphore_wait(barrier, len(smp_peers) + len(row_peers))
+    enter_start()
 
     def student(first, last):
         @pl.loop(first, last)
@@ -467,16 +480,26 @@
         gf_a(2)
         gf_a(3)
 
-    def mass_terms(h, first, last):
-        @pl.loop(first, last)
-        def _(j):
-            if h == 0:
-                for k in range(per):
-                    ls = slice(LANES * k, LANES * (k + 1))
-                    hi, lo = split(e[j, :, ls] * pscale[pl.ds(per * j + k, 1), :])
-                    dh[j, :, ls] = hi
-                    dl[j, :, ls] = lo
-            feat_terms(j, 0, everything)
+    def mass_tile(j, out):
+        for k in range(per):
+            ls = slice(LANES * k, LANES * (k + 1))
+            hi, lo = split(e[j, :, ls] * pscale[pl.ds(per * j + k, 1), :])
+            out[0, :, ls] = hi
+            out[1, :, ls] = lo
+
+    def mass_add(j, tile):
+        gfacc[0] += mm_t(tile[0], phl[j])
+        gfacc[0, :, 0:width] += mm_t(tile[1], phl[j, 0:width, :])
+
+    def mass_terms():
+        mass_tile(0, wa)
+
+        @pl.loop(0, tiles // 2)
+        def _(i):
+            mass_tile(2 * i + 1, wb)
+            mass_add(2 * i, wa)
+            mass_tile((2 * i + 2) % tiles, wa)
+            mass_add(2 * i + 1, wb)
 
     def mass_sum(h):
         rs = halves[h]
@@ -496,6 +519,7 @@
     peakf[...] = jnp.exp2(cola[0:half, :] - top)
 
     row_pass(0)
+    enter_wait()
     row_start(0)
     student(5, tiles)
     student_totals()
@@ -526,7 +550,7 @@
     row_start(2)
     gf_b(2)
     gf_b(3)
-    mass_terms(0, 0, tiles)
+    mass_terms()
     mass_sum(0)
     mass_sum(1)
     row_end(2)
@@ -534,10 +558,11 @@
     lag_core, lag_relay, lag_end = 2, 6, 10
     at = {
         2: [(gf_c, 2), (gf_c, 3)],
-        4: [(gf_c, 0)],
-        3: [(gf_b, 1)],
-        6: [(gf_d, 2), (gf_d, 3)],
-        5: [(gf_c, 1)],
+        3: [(gf_b, 0)],
+        4: [(gf_b, 1)],
+        5: [(gf_c, 0)],
+        6: [(gf_c, 1)],
+        7: [(gf_d, 2), (gf_d, 3)],
         9: [(gf_d, 0)],
         11: [(gf_d, 1)],
         12: [(gf_e, 0)],
@@ -562,7 +587,6 @@
         dlogits(i)
         gp_terms(i)
 
-    gf_b(0)
 
     @pl.loop(2, tiles + lag_end)
     def _(i):
@@ -666,6 +690,9 @@
         DMA((tiles,)),
         DMA((tiles, 6)),
         DMA((tiles, 6)),
+        pltpu.SemaphoreType.REGULAR,
+        V((2, rows, TILE), bf16),
+        V((2, rows, TILE), bf16),
     ]
     flops = 2 * rows * width * protos
     shapes = (

time: 89 us -> 88.4 us (level)
  no operation moved by 1% of the time
where the time goes in v5:
time: 88.4 us; the launch traced here: 88.3 us
  Pallas kernels  87.7 us (99%)
    pallas_call x1, Pallas kernels, local(): pl.pallas_call(functools.partial(kernel, SN, PN), out_shape=tuple((V(o.sh...  86.5 us

profile of v5, /device:TPU:1, one launch (start us, length us, event | category | flops | bytes accessed | tf_op | source)
XLA Modules:
  0.0 88.3 jit_solution(16279412609261441912)
XLA Ops:
  0.6 86.5 %shard_map.50 = (f32[512,384]{1,0:T(8,128)S(1)}, f32[48,4096]{1,0:T(8,128)S(1)}) custom-call(f32[512,384]{1,0:T(8,128)} %t_hbm.1, f32[512,384]{1,0:T(8,128)} %s_hbm.1, f32[384,4096]{1,0:T(8,128)} %p_hbm.1), custom_call_target="tpu_custom_call" | custom-call | flops 19327352832 | bytes 9437184 | tf_op jit(solution)/shard_map/pallas_call | solution.py:702
  87.2 1.2 %shard_map.51 = (f32[512,384]{1,0:T(8,128)}, f32[48,4096]{1,0:T(8,128)}) custom-call(f32[512,384]{1,0:T(8,128)S(1)} %get-tuple-element.4.gf_in, f32[48,4096]{1,0:T(8,128)S(1)} %get-tuple-element.5.gp_in), custom_call_target="tpu_custom_call" | custom-call | bytes 3145728 | tf_op jit(solution)/shard_map/pallas_call | solution.py:715

commit v6 on v5

--- a/solution.py
+++ b/solution.py
@@ -94,6 +94,8 @@
     enter_sem,
     wa,
     wb,
+    sa,
+    sb,
 ):
     ZN = PN // YN
     XN = SN // 2
@@ -176,20 +178,44 @@
     thh[:, width : 2 * width] = hi
     tl[...] = lo
 
-    @pl.loop(0, tiles)
-    def _(j):
-        load_p(j).wait()
+    def teacher_split(j):
         ph, plo = split(q[j, 0:width, :] * (1.0 / STUDENT_TEMP))
         phl[j, 0:width, :] = ph
         phl[j, width : 2 * width, :] = plo
-        scores = mm(thh[...], phl[j]) + mm(tl[...], phl[j, 0:width, :])
-        top = jnp.max(scores, axis=0, keepdims=True)
-        ex = jnp.exp2(scores - top)
+
+    def teacher_scores(j, out):
+        out[...] = mm(thh[...], phl[j]) + mm(tl[...], phl[j, 0:width, :])
+
+    def teacher_expo(j, scores):
+        top = jnp.max(scores[...], axis=0, keepdims=True)
+        ex = jnp.exp2(scores[...] - top)
         e[j] = ex
         total = jnp.sum(ex, axis=0, keepdims=True)
         for i in range(per):
             cola[pl.ds(per * j + i, 1), :] = top[:, LANES * i : LANES * (i + 1)]
             cola[pl.ds(per * (tiles + j) + i, 1), :] = total[:, LANES * i : LANES * (i + 1)]
+
+    load_p(0).wait()
+    load_p(1).wait()
+    teacher_split(0)
+    teacher_split(1)
+    teacher_scores(0, sa)
+
+    @pl.loop(0, tiles // 2 - 1)
+    def _(i):
+        j = 2 * i + 1
+        load_p(j + 1).wait()
+        load_p(j + 2).wait()
+        teacher_scores(j, sb)
+        teacher_expo(j - 1, sa)
+        teacher_split(j + 1)
+        teacher_scores(j + 1, sa)
+        teacher_expo(j, sb)
+        teacher_split(j + 2)
+
+    teacher_scores(tiles - 1, sb)
+    teacher_expo(tiles - 2, sa)
+    teacher_expo(tiles - 1, sb)
 
     enter_start()
 
@@ -693,6 +719,8 @@
         pltpu.SemaphoreType.REGULAR,
         V((2, rows, TILE), bf16),
         V((2, rows, TILE), bf16),
+        V((rows, TILE), f32),
+        V((rows, TILE), f32),
     ]
     flops = 2 * rows * width * protos
     shapes = (

time: 88.4 us -> 88.2 us (level)
  no operation moved by 1% of the time
where the time goes in v6:
time: 88.2 us; the launch traced here: 88.1 us
  Pallas kernels  87.5 us (99%)
    pallas_call x1, Pallas kernels, local(): pl.pallas_call(functools.partial(kernel, SN, PN), out_shape=tuple((V(o.sh...  86.3 us

profile of v6, /device:TPU:1, one launch (start us, length us, event | category | flops | bytes accessed | tf_op | source)
XLA Modules:
  0.0 88.1 jit_solution(15179244815276401338)
XLA Ops:
  0.6 86.3 %shard_map.50 = (f32[512,384]{1,0:T(8,128)S(1)}, f32[48,4096]{1,0:T(8,128)S(1)}) custom-call(f32[512,384]{1,0:T(8,128)} %t_hbm.1, f32[512,384]{1,0:T(8,128)} %s_hbm.1, f32[384,4096]{1,0:T(8,128)} %p_hbm.1), custom_call_target="tpu_custom_call" | custom-call | flops 19327352832 | bytes 9437184 | tf_op jit(solution)/shard_map/pallas_call | solution.py:730
  87.0 1.2 %shard_map.51 = (f32[512,384]{1,0:T(8,128)}, f32[48,4096]{1,0:T(8,128)}) custom-call(f32[512,384]{1,0:T(8,128)S(1)} %get-tuple-element.4.gf_in, f32[48,4096]{1,0:T(8,128)S(1)} %get-tuple-element.5.gp_in), custom_call_target="tpu_custom_call" | custom-call | bytes 3145728 | tf_op jit(solution)/shard_map/pallas_call | solution.py:743
